TPU v7x, 128 devices: a whole 4x4x4 slice. The times are simulated.
128 devices in a mesh: dp: 32 (over x, y, core), fsdp: 4 (over z).
Axes of the slice: x: 4, y: 4, z: 4, core: 2. Of those that a mesh axis runs over, the one named last changes fastest.
Arguments:
- tokens: bfloat16 [65536, 4608], P(('dp', 'fsdp')), as said below
- rmsnorm_gain_vector: bfloat16 [4608], replicated, may hold values from 0.099609375 to 1.8984375
- tied_query_matrix: bfloat16 [4608, 2048], P('fsdp'), may hold values from -0.09375 to 0.09375
- adapter_down_matrix: bfloat16 [4608, 128], P('fsdp'), may hold values from -0.09375 to 0.09375
- adapter_up_matrix: bfloat16 [128, 2048], replicated, may hold values from -0.5 to 0.5
- depth: int32 [4096], P(('dp', 'fsdp')), may hold values from 1 to 3, as said below
- destination: int32 [4096], P(('dp', 'fsdp')), may hold values from 0 to 31, as said below
- cotangent: bfloat16 [32768, 2048], P(('dp', 'fsdp')), may hold values from -6 to 6
Outputs:
- query: bfloat16 [32768, 2048], P(('dp', 'fsdp'))
- grad_tokens: bfloat16 [65536, 4608], P(('dp', 'fsdp'))
- grad_down: float32 [4608, 128], replicated
- grad_up: float32 [128, 2048], replicated
Inputs may be any that keep to these rules, and one draw needn't show every extreme that they name: Blocks that stop before this recursion have depth 1; the others have depth 2 or 3. `destination`: only entries of surviving blocks are read. Each dp index is named by exactly 16 surviving blocks with its own fsdp index, and by at most 1 surviving blocks of any one device; both bounds are reached in every draw. `tokens`: float values of mixed row and feature scales.
All inputs are finite; a program needn't handle non-finite values.
Results may differ from a plain program's by a relative error of at most 0.0053.
Values may be sent and summed in bfloat16 or wider, within the bound.
No kernel may reach another device: no remote copies, remote signals or barrier semaphores. Data moves between devices by JAX's collectives and lax.ppermute only.
A program may use at most 128 MiB of HBM per device.

v0:
```python
import jax
import jax.numpy as jnp
from jax import lax
from jax.sharding import PartitionSpec as P


def arrange(live, target, dp_count, slot_count):
    blocks = live.shape[0]
    order = jnp.arange(blocks, dtype=jnp.int32)
    same = (target[:, None] == target[None, :]) & live[None, :] & (order[None, :] < order[:, None])
    within = jnp.sum(same.astype(jnp.int32), axis=1)
    slot_of = target * slot_count + within
    places = jnp.arange(dp_count * slot_count, dtype=jnp.int32)
    hits = live[None, :] & (slot_of[None, :] == places[:, None])
    source = jnp.sum(jnp.where(hits, order[None, :], 0), axis=1)
    filled = jnp.any(hits, axis=1)
    return (slot_of, source, filled)


def compact(flags, capacity):
    count = flags.shape[0]
    rank = jnp.cumsum(flags.astype(jnp.int32)) - 1
    wanted = jnp.arange(capacity, dtype=jnp.int32)
    places = jnp.arange(count, dtype=jnp.int32)
    match = flags[None, :] & (rank[None, :] == wanted[:, None])
    pick = jnp.sum(jnp.where(match, places[None, :], 0), axis=1)
    return (pick, jnp.clip(rank, 0, capacity - 1))


def project_surviving(
    input_rows,
    incoming_gradient_rows,
    rmsnorm_gain_vector,
    tied_query_matrix,
    adapter_down_matrix,
    adapter_up_matrix,
):
    xfloat = input_rows.astype(jnp.float32)
    inverse = lax.rsqrt(jnp.mean(xfloat * xfloat, axis=-1, keepdims=True) + 1e-06)
    normed = xfloat * inverse
    gain_f = rmsnorm_gain_vector.astype(jnp.float32)
    normalized_blocks = (normed * gain_f).astype(jnp.bfloat16)
    full_weight, full_down = (
        lax.all_gather(tied_query_matrix, "fsdp", axis=0, tiled=True),
        lax.all_gather(adapter_down_matrix, "fsdp", axis=0, tiled=True),
    )
    shared_output = jnp.dot(normalized_blocks, full_weight, preferred_element_type=jnp.float32)
    lowrank_hidden = jnp.dot(
        normalized_blocks, full_down, preferred_element_type=jnp.float32
    ).astype(jnp.bfloat16)
    projected_query_rows = (
        shared_output
        + jnp.dot(lowrank_hidden, adapter_up_matrix, preferred_element_type=jnp.float32)
    ).astype(jnp.bfloat16)
    gradient_lowrank = jnp.einsum(
        "da,va->dv", incoming_gradient_rows, adapter_up_matrix, preferred_element_type=jnp.float32
    ).astype(jnp.bfloat16)
    gradient_normalized = jnp.einsum(
        "rq,dq->rd", incoming_gradient_rows, full_weight, preferred_element_type=jnp.float32
    )
    gradient_normalized = gradient_normalized + jnp.einsum(
        "rk,dk->rd", gradient_lowrank, full_down, preferred_element_type=jnp.float32
    )
    grad_up = jnp.einsum(
        "rk,rq->kq", lowrank_hidden, incoming_gradient_rows, preferred_element_type=jnp.float32
    )
    grad_down = jnp.einsum(
        "rd,rk->dk", normalized_blocks, gradient_lowrank, preferred_element_type=jnp.float32
    )
    dscaled = gradient_normalized * gain_f
    grad_rows = inverse * (dscaled - normed * jnp.mean(dscaled * normed, axis=-1, keepdims=True))
    return (projected_query_rows, grad_rows.astype(jnp.bfloat16), grad_down, grad_up)


def body(
    tokens,
    rmsnorm_gain_vector,
    tied_query_matrix,
    adapter_down_matrix,
    adapter_up_matrix,
    depth,
    destination,
    cotangent,
):
    dp_count = lax.axis_size("dp")
    blocks = depth.shape[0]
    block_rows = tokens.shape[0] // blocks
    width = tokens.shape[1]
    capacity = cotangent.shape[0] // block_rows
    slot_count = max(1, blocks // dp_count)
    live = depth >= 2
    slot_of, source, filled = arrange(live, destination, dp_count, slot_count)
    flag_send = filled.astype(jnp.bfloat16).reshape(dp_count, slot_count)
    zero_b = jnp.zeros((), jnp.bfloat16)
    token_blocks = tokens.reshape(blocks, block_rows, width)
    send_rows = jnp.where(filled[:, None, None], jnp.take(token_blocks, source, axis=0), zero_b)
    send_rows = send_rows.reshape(dp_count, slot_count, block_rows, width)
    got_rows, got_flags = (
        lax.all_to_all(send_rows, "dp", split_axis=0, concat_axis=0, tiled=True),
        lax.all_to_all(flag_send, "dp", split_axis=0, concat_axis=0, tiled=True),
    )
    flags = got_flags.reshape(-1) > 0.5
    pick, rank = compact(flags, capacity)
    input_rows = jnp.take(got_rows.reshape(dp_count * slot_count, block_rows, width), pick, axis=0)
    query, grad_rows, grad_down, grad_up = project_surviving(
        input_rows.reshape(capacity * block_rows, width),
        cotangent,
        rmsnorm_gain_vector,
        tied_query_matrix,
        adapter_down_matrix,
        adapter_up_matrix,
    )
    back = jnp.take(grad_rows.reshape(capacity, block_rows, width), rank, axis=0)
    back = jnp.where(flags[:, None, None], back, zero_b).reshape(
        dp_count, slot_count, block_rows, width
    )
    returned = lax.all_to_all(back, "dp", split_axis=0, concat_axis=0, tiled=True)
    grad_blocks = jnp.take(
        returned.reshape(dp_count * slot_count, block_rows, width), slot_of, axis=0
    )
    grad_tokens = jnp.where(live[:, None, None], grad_blocks, zero_b).reshape(
        tokens.shape[0], width
    )
    grad_down, grad_up = lax.psum((grad_down, grad_up), ("dp", "fsdp"))
    return (query, grad_tokens, grad_down, grad_up)


def solution(mesh):
    in_specs = (
        P(("dp", "fsdp"), None),
        P(),
        P("fsdp", None),
        P("fsdp", None),
        P(),
        P(("dp", "fsdp")),
        P(("dp", "fsdp")),
        P(("dp", "fsdp"), None),
    )
    out_specs = (P(("dp", "fsdp"), None), P(("dp", "fsdp"), None), P(), P())
    return jax.shard_map(body, mesh=mesh, in_specs=in_specs, out_specs=out_specs, check_vma=False)
```

profile of v0, /device:TPU:1, one launch (start us, length us, event | category | flops | bytes accessed | tf_op | source)
XLA Modules:
  0.0 448.2 jit_solution(3391662864419010734)
XLA Ops:
  7.2 0.0 copy-start
  7.2 0.0 copy-start.6
  7.2 0.0 copy-start.5
  7.2 0.0 all-gather.5.cloned.1.call-start
  7.2 0.7 all-gather.5.cloned.1.call-update
  7.9 0.0 all-gather.3.cloned.1.call-start
  8.0 0.7 all-gather.3.cloned.1.call-update
  8.7 0.0 copy-done.6
  8.7 0.0 copy-done.5
  8.7 0.2 convert_reduce_fusion
  8.9 0.1 fusion.7
  9.0 0.7 copy.18
  9.8 8.6 %all-to-all-start = ((bf16[32,1,1]{2,1,0:T(2,128)(2,1)}), bf16[32,1,1]{2,1,0:T(2,128)(2,1)S(1)}, u32[]{:S(2)}, u32[]{:S(2)}) async-start(bf16[32,1,1]{2,1,0:T(2,128)(2,1)} %copy.18), calls=%async_computation | async-start | bytes 32768 | tf_op jit(solution)/shard_map/all_to_all | solution.py:100
  18.4 0.1 select_reduce_fusion
  18.5 5.4 %gather_fusion.2 = bf16[32,16,4608]{2,1,0:T(8,128)(2,1)} fusion(bf16[32,16,4608]{2,1,0:T(8,128)(2,1)} %bitcast.43, s32[1024]{0:T(1024)S(1)} %pad_clamp_fusion.3), kind=kCustom, calls=%fused_computation.clone | custom fusion | bytes 9437312 | tf_op jit(solution)/shard_map/jit(_take)/gather | solution.py:96
  23.9 5.1 %fusion.2 = bf16[32,1,16,4608]{3,2,1,0:T(8,128)(2,1)} fusion(bf16[32,16,4608]{2,1,0:T(8,128)(2,1)} %gather_fusion.2, pred[32]{0:T(512)(128)(4,1)S(1)} %compare_and_fusion.1, pred[32]{0:T(512)(128)(4,1)S(1)} %fusion.7), kind=kLoop, calls=%fused_computation.10 | loop fusion | flops 4718592 | bytes 9437248 | tf_op jit(solution)/shard_map/reshape | solution.py:97
  29.0 0.0 copy-start.4
  29.0 0.0 copy-start.2
  29.0 0.0 all-to-all-done
  29.0 7.6 %all-to-all-start.1 = ((bf16[32,1,16,4608]{3,2,1,0:T(8,128)(2,1)}), bf16[32,1,16,4608]{3,2,1,0:T(8,128)(2,1)}, u32[]{:S(2)}, u32[]{:S(2)}) async-start(bf16[32,1,16,4608]{3,2,1,0:T(8,128)(2,1)} %fusion.2), calls=%async_computation.1 | async-start | bytes 9437184 | tf_op jit(solution)/shard_map/all_to_all | solution.py:99
  36.6 0.0 copy-done.4
  36.6 0.0 copy-done
  36.6 0.0 copy-done.2
  36.6 0.4 convolution_convert_fusion
  37.1 0.7 compare_reduce_fusion
  37.7 0.1 reduce-window.4
  37.8 0.1 fusion.4
  37.9 0.1 select_reduce_fusion.1
  38.0 0.1 broadcast_in_dim.107
  38.1 0.1 broadcast_in_dim.108
  38.2 0.0 all-gather.5.cloned.1.call-done
  38.3 4.3 fusion.11
  42.6 52.4 %all-to-all-done.1 = bf16[32,1,16,4608]{3,2,1,0:T(8,128)(2,1)} async-done(((bf16[32,1,16,4608]{3,2,1,0:T(8,128)(2,1)}), bf16[32,1,16,4608]{3,2,1,0:T(8,128)(2,1)}, u32[]{:S(2)}, u32[]{:S(2)}) %all-to-all-start.1) | async-done | bytes 4718624 | tf_op jit(solution)/shard_map/all_to_all | solution.py:99
  95.0 3.0 gather_fusion
  98.0 0.0 copy-start.1
  98.0 0.7 multiply_reduce_fusion.1
  98.8 0.1 rsqrt.12
  98.9 113.5 %all-gather.3.cloned.1.call-done = bf16[4608,2048]{1,0:T(8,128)(2,1)} async-done(((bf16[1152,2048]{1,0:T(8,128)(2,1)}), bf16[4608,2048]{1,0:T(8,128)(2,1)}) %all-gather.3.cloned.1.call-update) | async-done | bytes 18874384 | tf_op jit(solution)/shard_map/all_gather | solution.py:44
  212.4 12.0 %multiply_reduce_fusion = (f32[256]{0:T(256)S(1)}, f32[256,4608]{1,0:T(8,128)}) fusion(f32[256]{0:T(256)S(1)} %rsqrt.12, bf16[16,16,4608]{2,1,0:T(8,128)(2,1)S(1)} %gather_fusion, pred[256]{0:T(512)(128)(4,1)S(1)} %broadcast_in_dim.108, f32[4608]{0:T(1024)S(1)} %convert_element_type.61, f32[256,4608]{1,0:T(8,128)} %fusion.11, ...), kind=kOutput, calls=%fused_computation.12 | convolution fusion | flops 4840095744 | bytes 31740160 | tf_op jit(solution)/shard_map/rq,dq->rd/dot_general | solution.py:58
  224.4 0.0 copy-done.1
  224.4 6.4 %multiply_convert_fusion = (bf16[256,4608]{1,0:T(8,128)(2,1)}, bf16[256,4608]{1,0:T(8,128)(2,1)S(1)}) fusion(f32[256,4608]{1,0:T(8,128)} %get-tuple-element.16, f32[256]{0:T(256)S(1)} %broadcast_multiply_fusion, f32[256]{0:T(256)S(1)} %rsqrt.12, bf16[16,16,4608]{2,1,0:T(8,128)(2,1)} %copy-done.1, pred[256]{0:T(512)(128)(4,1)S(1)} %broadcast_in_dim.108, ...), kind=kLoop, calls=%fused_computation.11 | loop fusion | flops 10616832 | bytes 11817216 | tf_op jit(solution)/shard_map/convert_element_type | solution.py:72
  230.8 4.7 %gather_fusion.1 = bf16[32,16,4608]{2,1,0:T(8,128)(2,1)} fusion(bf16[16,16,4608]{2,1,0:T(8,128)(2,1)} %bitcast.42, s32[1024]{0:T(1024)S(1)} %pad_clamp_fusion.1), kind=kCustom, calls=%fused_computation.3 | custom fusion | bytes 9437312 | tf_op jit(solution)/shard_map/jit(_take)/gather | solution.py:113
  235.5 5.1 %fusion.1 = bf16[32,1,16,4608]{3,2,1,0:T(8,128)(2,1)} fusion(bf16[32,16,4608]{2,1,0:T(8,128)(2,1)} %gather_fusion.1, pred[32]{0:T(512)(128)(4,1)S(1)} %compare_and_fusion.2, pred[32]{0:T(512)(128)(4,1)S(1)} %get-tuple-element.13), kind=kLoop, calls=%fused_computation.7 | loop fusion | flops 4718592 | bytes 9437248 | tf_op jit(solution)/shard_map/jit(_where)/select_n | solution.py:114
  240.6 7.6 %all-to-all-start.2 = ((bf16[32,1,16,4608]{3,2,1,0:T(8,128)(2,1)}), bf16[32,1,16,4608]{3,2,1,0:T(8,128)(2,1)}, u32[]{:S(2)}, u32[]{:S(2)}) async-start(bf16[32,1,16,4608]{3,2,1,0:T(8,128)(2,1)} %fusion.1), calls=%async_computation.2 | async-start | bytes 9437184 | tf_op jit(solution)/shard_map/all_to_all | solution.py:117
  248.2 0.2 all-reduce.3.cloned.1.call-start
  248.5 2.0 convolution_convert_fusion.1
  250.5 1.3 fusion.13
  251.8 2.2 fusion.12
  254.1 0.0 all-reduce.3.cloned.1.call-update
  254.1 1.5 fusion.10
  255.5 10.5 %fusion.3 = bf16[256,2048]{1,0:T(8,128)(2,1)} fusion(f32[256,2048]{1,0:T(8,128)S(1)} %fusion.10, bf16[256,4608]{1,0:T(8,128)(2,1)S(1)} %get-tuple-element.12, bf16[4608,2048]{1,0:T(8,128)(2,1)} %all-gather.3.cloned.1.call-done), kind=kOutput, calls=%fused_computation.17 | convolution fusion | flops 4832886784 | bytes 24379392 | tf_op jit(solution)/shard_map/dot_general | solution.py:47
  266.0 44.1 %all-to-all-done.2 = bf16[32,1,16,4608]{3,2,1,0:T(8,128)(2,1)} async-done(((bf16[32,1,16,4608]{3,2,1,0:T(8,128)(2,1)}), bf16[32,1,16,4608]{3,2,1,0:T(8,128)(2,1)}, u32[]{:S(2)}, u32[]{:S(2)}) %all-to-all-start.2) | async-done | bytes 4718624 | tf_op jit(solution)/shard_map/all_to_all | solution.py:117
  310.2 5.4 %gather_fusion.3 = bf16[32,16,4608]{2,1,0:T(8,128)(2,1)} fusion(bf16[32,16,4608]{2,1,0:T(8,128)(2,1)} %bitcast.10, s32[1024]{0:T(1024)S(1)} %pad_clamp_fusion), kind=kCustom, calls=%fused_computation.1.clone | custom fusion | bytes 9437312 | tf_op jit(solution)/shard_map/jit(_take)/gather | solution.py:118
  315.6 5.2 %select_select_fusion = bf16[32,16,4608]{2,1,0:T(8,128)(2,1)} fusion(bf16[32,16,4608]{2,1,0:T(8,128)(2,1)} %gather_fusion.3, pred[32]{0:T(512)(128)(4,1)S(1)} %get-tuple-element.9, pred[32]{0:T(512)(128)(4,1)S(1)} %broadcast_compare_fusion), kind=kLoop, calls=%fused_computation.8 | loop fusion | flops 4718592 | bytes 9437248 | tf_op jit(solution)/shard_map/jit(_where)/select_n | solution.py:121
  320.8 116.6 %all-reduce.3.cloned.1.call-done = (f32[4608,128]{1,0:T(8,128)}, f32[128,2048]{1,0:T(8,128)}) async-done(((f32[4608,128]{1,0:T(8,128)}, f32[128,2048]{1,0:T(8,128)}), (f32[4608,128]{1,0:T(8,128)}, f32[128,2048]{1,0:T(8,128)})) %all-reduce.3.cloned.1.call-update) | async-done | bytes 3407888 | tf_op jit(solution)/shard_map/psum | solution.py:124
  437.4 0.0 copy-start.3
  437.4 3.3 copy.22
  440.7 0.0 copy-done.3
  440.7 1.0 copy.23
  (16 shorter events, 0.1 us)
Async XLA Ops:
  7.2 29.4 %copy-start = (bf16[256,2048]{1,0:T(8,128)(2,1)S(1)}, bf16[256,2048]{1,0:T(8,128)(2,1)}, u32[]{:S(2)}) copy-start(bf16[256,2048]{1,0:T(8,128)(2,1)} %param.17) | copy-start | bytes 3145732
  7.2 1.5 copy-start.6
  7.2 1.5 copy-start.5
  7.2 31.1 %all-gather.5.cloned.1.call-start = ((), (), s32[]{:S(2)}) async-start(), calls=%async_computation.4 | async-start | bytes 1474560 | tf_op jit(solution)/shard_map/all_gather | solution.py:45
  7.9 204.4 %all-gather.3.cloned.1.call-start = ((), (), s32[]{:S(2)}) async-start(), calls=%async_computation.3 | async-start | bytes 23592960 | tf_op jit(solution)/shard_map/all_gather | solution.py:44
  9.8 19.2 %all-to-all-start = ((bf16[32,1,1]{2,1,0:T(2,128)(2,1)}), bf16[32,1,1]{2,1,0:T(2,128)(2,1)S(1)}, u32[]{:S(2)}, u32[]{:S(2)}) async-start(bf16[32,1,1]{2,1,0:T(2,128)(2,1)} %copy.18), calls=%async_computation | async-start | bytes 32768 | tf_op jit(solution)/shard_map/all_to_all | solution.py:100
  29.0 7.6 %copy-start.4 = (bf16[4608]{0:T(1024)(128)(2,1)S(1)}, bf16[4608]{0:T(1024)(128)(2,1)}, u32[]{:S(2)}) copy-start(bf16[4608]{0:T(1024)(128)(2,1)} %param.11) | copy-start | bytes 27652
  29.0 7.6 %copy-start.2 = (bf16[128,2048]{1,0:T(8,128)(2,1)S(1)}, bf16[128,2048]{1,0:T(8,128)(2,1)}, u32[]{:S(2)}) copy-start(bf16[128,2048]{1,0:T(8,128)(2,1)} %param.14) | copy-start | bytes 1572868
  29.0 66.0 %all-to-all-start.1 = ((bf16[32,1,16,4608]{3,2,1,0:T(8,128)(2,1)}), bf16[32,1,16,4608]{3,2,1,0:T(8,128)(2,1)}, u32[]{:S(2)}, u32[]{:S(2)}) async-start(bf16[32,1,16,4608]{3,2,1,0:T(8,128)(2,1)} %fusion.2), calls=%async_computation.1 | async-start | bytes 9437184 | tf_op jit(solution)/shard_map/all_to_all | solution.py:99
  98.0 126.4 %copy-start.1 = (bf16[16,16,4608]{2,1,0:T(8,128)(2,1)}, bf16[16,16,4608]{2,1,0:T(8,128)(2,1)S(1)}, u32[]{:S(2)}) copy-start(bf16[16,16,4608]{2,1,0:T(8,128)(2,1)S(1)} %gather_fusion) | copy-start | bytes 7077892
  240.6 69.6 %all-to-all-start.2 = ((bf16[32,1,16,4608]{3,2,1,0:T(8,128)(2,1)}), bf16[32,1,16,4608]{3,2,1,0:T(8,128)(2,1)}, u32[]{:S(2)}, u32[]{:S(2)}) async-start(bf16[32,1,16,4608]{3,2,1,0:T(8,128)(2,1)} %fusion.1), calls=%async_computation.2 | async-start | bytes 9437184 | tf_op jit(solution)/shard_map/all_to_all | solution.py:117
  248.2 189.1 %all-reduce.3.cloned.1.call-start = ((), (), s32[]{:S(2)}) async-start(), calls=%async_computation.5 | async-start | bytes 6815744 | tf_op jit(solution)/shard_map/psum | solution.py:124
  437.4 3.3 copy-start.3
Sparse Core Ops, SparseCore 0:
  9.7 26.8 all-gather.4
  38.3 174.0 all-gather.2
  254.7 182.6 all-reduce.2
where the time goes:
time: 449 us; the launch traced here: 448 us
  waiting for transfers between devices  328 us (73%)
  matrix products  34.3 us (8%)
  other arithmetic  24.1 us (5%)
  starting transfers between devices  24 us (5%)
  local copies, waits for them, and re-layouts  23.8 us (5%)
  between operations  14 us (3%)
    psum x1, waiting for transfers between devices, body(): grad_down, grad_up = lax.psum((grad_down, grad_up), ('dp', 'fsdp'))  117 us
    all_gather x1, waiting for transfers between devices, project_surviving(): lax.all_gather(tied_query_matrix, 'fsdp', axis=0, tiled=True)  113 us
    all_to_all x1, waiting for transfers between devices, body(): lax.all_to_all(send_rows, 'dp', split_axis=0, concat_axis=0, tiled=True)  52.4 us
    all_to_all x1, waiting for transfers between devices, body(): lax.all_to_all(back, 'dp', split_axis=0, concat_axis=0, tiled=True)  44.1 us
    dot_general x1, matrix products, project_surviving(): jnp.einsum('rq,dq->rd', incoming_gradient_rows, full_weight, preferred_el...  12 us
    dot_general x1, matrix products, project_surviving(): jnp.dot(normalized_blocks, full_weight, preferred_element_type=jnp.float32)  10.5 us
  transfers between devices with their start and end apart: 6, of which 4 were waited for; matrix products, arithmetic and copies ran while one was open for 11% of the time, Pallas kernels for 0%

commit v1 on v0

--- a/solution.py
+++ b/solution.py
@@ -41,7 +41,10 @@
     gain_f = rmsnorm_gain_vector.astype(jnp.float32)
     normalized_blocks = (normed * gain_f).astype(jnp.bfloat16)
     full_weight, full_down = (
-        lax.all_gather(tied_query_matrix, "fsdp", axis=0, tiled=True),
+        jnp.concatenate(
+            lax.all_to_all(jnp.stack([tied_query_matrix] * lax.axis_size("fsdp")), "fsdp", 0, 0),
+            axis=0,
+        ),
         lax.all_gather(adapter_down_matrix, "fsdp", axis=0, tiled=True),
     )
     shared_output = jnp.dot(normalized_blocks, full_weight, preferred_element_type=jnp.float32)

time: 449 us -> 556 us (1.24)
  blocking collectives: 0 us -> 64.3 us
  waiting for transfers between devices: 328 us -> 365 us
    all_to_all x1, waiting for transfers between devices: 52.4 us -> 175 us  [project_surviving(): lax.all_to_all(jnp.stack([tied_query_matrix] * lax.axis_size('fsdp')), 'f...]
    all_gather x1 -> x0, waiting for transfers between devices: 113 us -> none  [project_surviving(): lax.all_gather(tied_query_matrix, 'fsdp', axis=0, tiled=True)]
    all_to_all x0 -> x1, blocking collectives: none -> 64.3 us  [body(): lax.all_to_all(send_rows, 'dp', split_axis=0, concat_axis=0, tiled=True)]
    all_gather x1, waiting for transfers between devices: 0.02 us -> 31.7 us  [project_surviving(): lax.all_gather(adapter_down_matrix, 'fsdp', axis=0, tiled=True)]
    another operation x0 -> x1, local copies, waits for them, and re-layouts: none -> 6.84 us  [project_surviving(): jnp.stack([tied_query_matrix] * lax.axis_size('fsdp'))]
  transfers between devices with their start and end apart: 6 -> 5, of which waited for: 4 -> 4; matrix products, arithmetic and copies ran while one was open for 11% -> 9% of each run, Pallas kernels for 0% -> 0%
where the time goes in v1:
time: 556 us; the launch traced here: 555 us
  waiting for transfers between devices  365 us (66%)
  blocking collectives  64.3 us (12%)
  matrix products  34.1 us (6%)
  local copies, waits for them, and re-layouts  29.1 us (5%)
  other arithmetic  26.4 us (5%)
  starting transfers between devices  21.3 us (4%)
  between operations  14.3 us (3%)
    all_to_all x1, waiting for transfers between devices, project_surviving(): lax.all_to_all(jnp.stack([tied_query_matrix] * lax.axis_size('fsdp')), 'f...  175 us
    psum x1, waiting for transfers between devices, body(): grad_down, grad_up = lax.psum((grad_down, grad_up), ('dp', 'fsdp'))  116 us
    all_to_all x1, blocking collectives, body(): lax.all_to_all(send_rows, 'dp', split_axis=0, concat_axis=0, tiled=True)  64.3 us
    all_to_all x1, waiting for transfers between devices, body(): lax.all_to_all(back, 'dp', split_axis=0, concat_axis=0, tiled=True)  42.2 us
    all_gather x1, waiting for transfers between devices, project_surviving(): lax.all_gather(adapter_down_matrix, 'fsdp', axis=0, tiled=True)  31.7 us
    dot_general x1, matrix products, project_surviving(): jnp.einsum('rq,dq->rd', incoming_gradient_rows, full_weight, preferred_el...  12.4 us
  transfers between devices with their start and end apart: 5, of which 4 were waited for; matrix products, arithmetic and copies ran while one was open for 9% of the time, Pallas kernels for 0%

profile of v1, /device:TPU:1, one launch (start us, length us, event | category | flops | bytes accessed | tf_op | source)
XLA Modules:
  0.0 554.9 jit_solution(6331547685246185587)
XLA Ops:
  7.2 0.0 copy-start
  7.2 0.7 broadcast_compare_fusion
  7.9 0.9 convert_reduce_fusion
  8.8 0.7 compare_and_fusion
  9.5 0.1 fusion.11
  9.6 0.7 copy.18
  10.4 8.6 %all-to-all-start = ((bf16[32,1,1]{2,1,0:T(2,128)(2,1)}), bf16[32,1,1]{2,1,0:T(2,128)(2,1)S(1)}, u32[]{:S(2)}, u32[]{:S(2)}) async-start(bf16[32,1,1]{2,1,0:T(2,128)(2,1)} %copy.18), calls=%async_computation | async-start | bytes 32768 | tf_op jit(solution)/shard_map/all_to_all | solution.py:103
  18.9 0.1 select_reduce_fusion
  19.1 5.4 gather_fusion.2
  24.5 5.1 fusion.5
  29.6 0.0 all-to-all-done
  29.6 0.0 copy-start.4
  29.6 64.3 %all_to_all.21 = bf16[32,1,16,4608]{3,2,1,0:T(8,128)(2,1)} all-to-all(bf16[32,1,16,4608]{3,2,1,0:T(8,128)(2,1)} %fusion.5), channel_id=1, replica_groups=mesh['dp'=32,'fsdp'=4] {'dp'}, dimensions={0} | all-to-all | bytes 9437184 | tf_op jit(solution)/shard_map/all_to_all | solution.py:102
  93.9 0.0 copy-done.4
  93.9 6.8 %stack.2 = bf16[4,1152,2048]{2,1,0:T(8,128)(2,1)} broadcast(bf16[1152,2048]{1,0:T(8,128)(2,1)S(1)} %copy-done.4), dimensions={1,2} | broadcast | bytes 23592960 | tf_op jit(solution)/shard_map/stack | solution.py:45
  100.7 7.5 %all-to-all-start.2 = ((bf16[4,1152,2048]{2,1,0:T(8,128)(2,1)}), bf16[4,1152,2048]{2,1,0:T(8,128)(2,1)}, u32[]{:S(2)}, u32[]{:S(2)}) async-start(bf16[4,1152,2048]{2,1,0:T(8,128)(2,1)} %stack.2), calls=%async_computation.2 | async-start | bytes 37748736 | tf_op jit(solution)/shard_map/all_to_all | solution.py:45
  108.2 0.0 all-gather.2.cloned.1.call-start
  108.3 0.7 all-gather.2.cloned.1.call-update
  109.0 0.0 copy-done.10
  109.0 0.0 copy-done
  109.0 0.0 copy-done.6
  109.0 0.4 convolution_convert_fusion
  109.4 0.7 compare_reduce_fusion
  110.1 0.1 reduce-window.4
  110.2 0.1 fusion.8
  110.3 0.1 select_reduce_fusion.1
  110.4 0.1 broadcast_in_dim.112
  110.5 0.1 broadcast_in_dim.113
  110.6 31.7 %all-gather.2.cloned.1.call-done = bf16[4608,128]{1,0:T(8,128)(2,1)} async-done(((bf16[1152,128]{1,0:T(8,128)(2,1)}), bf16[4608,128]{1,0:T(8,128)(2,1)}) %all-gather.2.cloned.1.call-update) | async-done | bytes 1179664 | tf_op jit(solution)/shard_map/all_gather | solution.py:48
  142.3 4.2 fusion.15
  146.6 3.0 gather_fusion
  149.6 0.0 copy-start.1
  149.6 0.7 fusion.1
  150.4 0.1 rsqrt.13
  150.5 174.6 %all-to-all-done.2 = bf16[4,1152,2048]{2,1,0:T(8,128)(2,1)} async-done(((bf16[4,1152,2048]{2,1,0:T(8,128)(2,1)}), bf16[4,1152,2048]{2,1,0:T(8,128)(2,1)}, u32[]{:S(2)}, u32[]{:S(2)}) %all-to-all-start.2) | async-done | bytes 18874400 | tf_op jit(solution)/shard_map/all_to_all | solution.py:45
  325.0 12.4 %multiply_reduce_fusion = (f32[256]{0:T(256)S(1)}, bf16[256,4608]{1,0:T(8,128)(2,1)}, f32[256,4608]{1,0:T(8,128)}) fusion(f32[256]{0:T(256)S(1)} %rsqrt.13, bf16[16,16,4608]{2,1,0:T(8,128)(2,1)S(1)} %gather_fusion, pred[256]{0:T(512)(128)(4,1)S(1)} %broadcast_in_dim.113, f32[4608]{0:T(1024)S(1)} %convert_element_type.78, f32[256,4608]{1,0:T(8,128)} %fusion.15, ...), kind=kOutput, calls=%fused_computation.17 | convolution fusion | flops 4840095744 | bytes 34099456 | tf_op jit(solution)/shard_map/rq,dq->rd/dot_general | solution.py:61
  337.4 0.0 copy-done.1
  337.4 4.3 multiply_convert_fusion
  341.7 3.0 gather_fusion.1
  344.8 5.1 fusion.4
  349.9 5.0 all-to-all-start.3
  354.9 0.2 all-reduce.3.cloned.1.call-start
  355.1 0.0 copy-start.3
  355.1 0.0 copy-start.7
  355.2 0.0 copy-done.2
  355.2 2.3 fusion.3
  357.5 0.0 copy-done.3
  357.5 0.0 copy-done.7
  357.5 0.9 convolution_convert_fusion.1
  358.4 0.0 copy-start.9
  358.5 1.3 fusion.16
  359.8 0.0 copy-done.9
  359.8 2.4 fusion.7
  362.2 0.0 all-reduce.3.cloned.1.call-update
  362.2 1.6 fusion.14
  363.9 0.2 copy-done.5
  364.1 10.8 %fusion.6 = bf16[256,2048]{1,0:T(8,128)(2,1)} fusion(f32[256,2048]{1,0:T(8,128)S(1)} %fusion.14, bf16[256,4608]{1,0:T(8,128)(2,1)S(1)} %bitcast.41, bf16[4608,2048]{1,0:T(8,128)(2,1)} %bitcast.8), kind=kOutput, calls=%fused_computation.21 | convolution fusion | flops 4832886784 | bytes 24379392 | tf_op jit(solution)/shard_map/dot_general | solution.py:50
  374.8 42.2 %all-to-all-done.3 = bf16[32,1,16,4608]{3,2,1,0:T(8,128)(2,1)} async-done(((bf16[32,1,16,4608]{3,2,1,0:T(8,128)(2,1)}), bf16[32,1,16,4608]{3,2,1,0:T(8,128)(2,1)}, u32[]{:S(2)}, u32[]{:S(2)}) %all-to-all-start.3) | async-done | bytes 4718624 | tf_op jit(solution)/shard_map/all_to_all | solution.py:120
  417.0 5.4 gather_fusion.3
  422.4 5.2 select_select_fusion
  427.6 116.2 %all-reduce.3.cloned.1.call-done = (f32[4608,128]{1,0:T(8,128)}, f32[128,2048]{1,0:T(8,128)}) async-done(((f32[4608,128]{1,0:T(8,128)}, f32[128,2048]{1,0:T(8,128)}), (f32[4608,128]{1,0:T(8,128)}, f32[128,2048]{1,0:T(8,128)})) %all-reduce.3.cloned.1.call-update) | async-done | bytes 3407888 | tf_op jit(solution)/shard_map/psum | solution.py:127
  543.8 3.3 copy.22
  547.1 0.0 copy-done.8
  547.1 1.0 copy.23
  (19 shorter events, 0.1 us)
Async XLA Ops:
  7.2 101.8 %copy-start = (bf16[256,2048]{1,0:T(8,128)(2,1)S(1)}, bf16[256,2048]{1,0:T(8,128)(2,1)}, u32[]{:S(2)}) copy-start(bf16[256,2048]{1,0:T(8,128)(2,1)} %param.17) | copy-start | bytes 3145732
  10.4 19.2 %all-to-all-start = ((bf16[32,1,1]{2,1,0:T(2,128)(2,1)}), bf16[32,1,1]{2,1,0:T(2,128)(2,1)S(1)}, u32[]{:S(2)}, u32[]{:S(2)}) async-start(bf16[32,1,1]{2,1,0:T(2,128)(2,1)} %copy.18), calls=%async_computation | async-start | bytes 32768 | tf_op jit(solution)/shard_map/all_to_all | solution.py:103
  29.6 64.3 %copy-start.4 = (bf16[1152,2048]{1,0:T(8,128)(2,1)S(1)}, bf16[1152,2048]{1,0:T(8,128)(2,1)}, u32[]{:S(2)}) copy-start(bf16[1152,2048]{1,0:T(8,128)(2,1)} %param.12) | copy-start | bytes 14155780
  100.7 8.2 %copy-start.10 = (bf16[4608]{0:T(1024)(128)(2,1)S(1)}, bf16[4608]{0:T(1024)(128)(2,1)}, u32[]{:S(2)}) copy-start(bf16[4608]{0:T(1024)(128)(2,1)} %param.11) | copy-start | bytes 27652
  100.7 8.3 %copy-start.6 = (bf16[128,2048]{1,0:T(8,128)(2,1)S(1)}, bf16[128,2048]{1,0:T(8,128)(2,1)}, u32[]{:S(2)}) copy-start(bf16[128,2048]{1,0:T(8,128)(2,1)} %param.14) | copy-start | bytes 1572868
  100.7 224.3 %all-to-all-start.2 = ((bf16[4,1152,2048]{2,1,0:T(8,128)(2,1)}), bf16[4,1152,2048]{2,1,0:T(8,128)(2,1)}, u32[]{:S(2)}, u32[]{:S(2)}) async-start(bf16[4,1152,2048]{2,1,0:T(8,128)(2,1)} %stack.2), calls=%async_computation.2 | async-start | bytes 37748736 | tf_op jit(solution)/shard_map/all_to_all | solution.py:45
  108.2 34.1 %all-gather.2.cloned.1.call-start = ((), (), s32[]{:S(2)}) async-start(), calls=%async_computation.4 | async-start | bytes 1474560 | tf_op jit(solution)/shard_map/all_gather | solution.py:48
  149.6 187.8 %copy-start.1 = (bf16[16,16,4608]{2,1,0:T(8,128)(2,1)}, bf16[16,16,4608]{2,1,0:T(8,128)(2,1)S(1)}, u32[]{:S(2)}) copy-start(bf16[16,16,4608]{2,1,0:T(8,128)(2,1)S(1)} %gather_fusion) | copy-start | bytes 7077892
  349.9 5.3 copy-start.2
  349.9 67.1 %all-to-all-start.3 = ((bf16[32,1,16,4608]{3,2,1,0:T(8,128)(2,1)}), bf16[32,1,16,4608]{3,2,1,0:T(8,128)(2,1)}, u32[]{:S(2)}, u32[]{:S(2)}) async-start(bf16[32,1,16,4608]{3,2,1,0:T(8,128)(2,1)} %fusion.4), calls=%async_computation.3 | async-start | bytes 9437184 | tf_op jit(solution)/shard_map/all_to_all | solution.py:120
  354.9 188.9 %all-reduce.3.cloned.1.call-start = ((), (), s32[]{:S(2)}) async-start(), calls=%async_computation.5 | async-start | bytes 6815744 | tf_op jit(solution)/shard_map/psum | solution.py:127
  355.1 2.4 copy-start.3
  355.1 2.4 copy-start.7
  358.4 1.3 copy-start.9
  362.2 1.9 copy-start.5
  543.8 3.3 copy-start.8
Sparse Core Ops, SparseCore 0:
  110.7 31.5 all-gather.1
  362.4 181.3 all-reduce.2
